TPU v7x, 512 devices: a whole 4x8x8 slice. The times are simulated.
512 devices in a mesh: table: 32 (over y_hi, z), dp: 16 (over x, y_lo, core).
Axes of the slice: x: 4, y: 8 (y_hi: 4, y_lo: 2; y = y_hi * 2 + y_lo), z: 8, core: 2. Of those that a mesh axis runs over, the one named last changes fastest.
Arguments:
- features: bfloat16 [6144, 131072], P('dp', 'table'), may hold values from -6 to 6
- weight: bfloat16 [131072, 256], P(('table', 'dp')), may hold values from -0.015625 to 0.015625
- moment_one: float32 [131072, 256], P(('table', 'dp')), may hold values from -6 to 6
- moment_two: float32 [131072, 256], P(('table', 'dp')), may hold values from 1 to 10
- cotangent: bfloat16 [6144, 256], P('dp'), may hold values from -0.375 to 0.375
Outputs:
- hidden: bfloat16 [6144, 256], P(('dp', 'table'))
- new_moment_one: float32 [131072, 256], P(('table', 'dp'))
- new_moment_two: float32 [131072, 256], P(('table', 'dp'))
- direction: float32 [131072, 256], P(('table', 'dp'))
All inputs are finite; a program needn't handle non-finite values.
Results may differ from a plain program's by a relative error of at most 0.0025.
Values may be sent and summed in bfloat16 or wider, within the bound.
A program may use at most 64 MiB of HBM per device.

v0:
```python
import jax
import jax.numpy as jnp
from jax import lax
from jax.sharding import PartitionSpec as P

bias_one = 0.99997343860111
bias_two = 0.63396765872677


def silu_slope(pre):
    sigma = jax.nn.sigmoid(pre)
    return sigma * (1.0 + pre * (1.0 - sigma))


def shards(features, weight, moment_one, moment_two, cotangent):
    samples = features.shape[0]
    columns = features
    partial_value = jnp.dot(
        columns,
        lax.all_gather(weight, "dp", axis=0, tiled=True),
        preferred_element_type=jnp.float32,
    )
    own_rows = samples // lax.axis_size("table")
    first_own = lax.axis_index("table") * own_rows
    pre_all = lax.psum(partial_value, "table")
    pre = lax.dynamic_slice_in_dim(pre_all, first_own, own_rows, 0)
    hidden = jax.nn.silu(pre).astype(jnp.bfloat16)
    slope_all = (cotangent.astype(jnp.float32) * silu_slope(pre_all)).astype(jnp.bfloat16)
    columns = features
    grad = lax.psum_scatter(
        lax.dot_general(
            columns, slope_all, (((0,), (0,)), ((), ())), preferred_element_type=jnp.float32
        ),
        "dp",
        scatter_dimension=0,
        tiled=True,
    )
    new_moment_one = 0.9 * moment_one + 0.1 * grad
    new_moment_two = 0.99 * moment_two + 0.01 * grad * grad
    direction = new_moment_one / bias_one / (jnp.sqrt(new_moment_two / bias_two) + 1e-08)
    return (hidden, new_moment_one, new_moment_two, direction)


def solution(mesh):
    return jax.shard_map(
        shards,
        mesh=mesh,
        in_specs=(
            P("dp", "table"),
            P(("table", "dp"), None),
            P(("table", "dp"), None),
            P(("table", "dp"), None),
            P("dp", None),
        ),
        out_specs=(
            P(("dp", "table"), None),
            P(("table", "dp"), None),
            P(("table", "dp"), None),
            P(("table", "dp"), None),
        ),
        check_vma=False,
    )
```

profile of v0, /device:TPU:1, one launch (start us, length us, event | category | flops | bytes accessed | tf_op | source)
XLA Modules:
  0.0 448.1 jit_solution(3819247086145248978)
XLA Ops:
  7.2 0.0 copy-start
  7.2 0.0 all-gather.2.cloned.1.call-start
  7.2 0.7 all-gather.2.cloned.1.call-update
  7.9 0.0 copy-start.1
  7.9 0.0 all-reduce.2.cloned.1.call-start
  8.0 47.4 %all-gather.2.cloned.1.call-done = bf16[4096,256]{1,0:T(8,128)(2,1)} async-done(((bf16[256,256]{1,0:T(8,128)(2,1)}), bf16[4096,256]{1,0:T(8,128)(2,1)}) %all-gather.2.cloned.1.call-update) | async-done | bytes 2097168 | tf_op jit(solution)/shard_map/all_gather | solution.py:20
  55.4 0.0 copy-done
  55.4 3.3 fusion.4
  58.7 0.0 all-reduce.2.cloned.1.call-update
  58.8 0.0 reduce-scatter.2.cloned.1.call-start
  58.8 283.5 %all-reduce.2.cloned.1.call-done = f32[384,256]{1,0:T(8,128)} async-done(((f32[384,256]{1,0:T(8,128)}), f32[384,256]{1,0:T(8,128)}) %all-reduce.2.cloned.1.call-update) | async-done | bytes 393232 | tf_op jit(solution)/shard_map/psum | solution.py:25
  342.3 0.0 copy-done.1
  342.3 4.3 convolution_bitcast_fusion
  346.6 0.0 reduce-scatter.2.cloned.1.call-update
  346.7 1.1 copy.10
  347.8 1.8 copy.9
  349.5 1.4 multiply_convert_fusion.2
  350.9 83.3 %reduce-scatter.2.cloned.1.call-done = f32[256,256]{0,1:T(8,128)} async-done(((f32[4096,256]{0,1:T(8,128)}), f32[256,256]{0,1:T(8,128)}) %reduce-scatter.2.cloned.1.call-update) | async-done | bytes 262160 | tf_op jit(solution)/shard_map/reduce_scatter | solution.py:30
  434.2 2.0 add_divide_fusion
  436.2 1.8 copy.11
  438.0 1.8 copy.12
  439.8 1.8 copy.13
Async XLA Ops:
  7.2 48.3 %copy-start = (bf16[384,4096]{1,0:T(8,128)(2,1)S(1)}, bf16[384,4096]{1,0:T(8,128)(2,1)}, u32[]{:S(2)}) copy-start(bf16[384,4096]{1,0:T(8,128)(2,1)} %param.5) | copy-start | bytes 9437188
  7.2 48.2 %all-gather.2.cloned.1.call-start = ((), (), s32[]{:S(2)}) async-start(), calls=%async_computation.1 | async-start | bytes 2228224 | tf_op jit(solution)/shard_map/all_gather | solution.py:20
  7.9 334.4 %copy-start.1 = (bf16[384,256]{1,0:T(8,128)(2,1)S(1)}, bf16[384,256]{1,0:T(8,128)(2,1)}, u32[]{:S(2)}) copy-start(bf16[384,256]{1,0:T(8,128)(2,1)} %param.9) | copy-start | bytes 589828
  7.9 334.4 %all-reduce.2.cloned.1.call-start = ((), (), s32[]{:S(2)}) async-start(), calls=%async_computation.2 | async-start | bytes 786432 | tf_op jit(solution)/shard_map/psum | solution.py:25
  58.8 375.5 %reduce-scatter.2.cloned.1.call-start = ((), (), s32[]{:S(2)}) async-start(), calls=%async_computation.3 | async-start | bytes 4456448 | tf_op jit(solution)/shard_map/reduce_scatter | solution.py:30
Sparse Core Ops, SparseCore 0:
  10.2 45.2 all-gather.1
  58.9 283.4 all-reduce.1
  346.8 87.3 reduce-scatter.1
where the time goes:
time: 450 us; the launch traced here: 448 us
  waiting for transfers between devices  415 us (92%)
  between operations  13.8 us (3%)
  local copies, waits for them, and re-layouts  8.24 us (2%)
  matrix products  7.61 us (2%)
    psum x1, waiting for transfers between devices, shards(): pre_all = lax.psum(partial_value, 'table')  284 us
    reduce_scatter x1, waiting for transfers between devices, shards(): lax.psum_scatter(lax.dot_general(columns, slope_all, (((0,), (0,)), ((),...  83.3 us
    all_gather x1, waiting for transfers between devices, shards(): lax.all_gather(weight, 'dp', axis=0, tiled=True)  47.4 us
  transfers between devices with their start and end apart: 3, of which 3 were waited for; matrix products, arithmetic and copies ran while one was open for 1% of the time, Pallas kernels for 0%

commit v1 on v0

v1 whole, which is shorter than its diff:
```python
import jax
import jax.numpy as jnp
from jax import lax
from jax.experimental import pallas as pl
from jax.experimental.pallas import tpu as pltpu
from jax.sharding import PartitionSpec as P

bias_one = 0.99997343860111
bias_two = 0.63396765872677

NX, NY, NC = 4, 2, 2
NU, NZ = 4, 8
LANES = NX * NY
HALVES, COLS = 2, 128
ROWS, DEPTH = 384, 256
OWN = ROWS // (NU * NZ)
PACK = OWN * NU
ORDER = (5, 4, 3, 7, 2, 6, 1)
ZORDER = (4, 3, 5, 2, 6, 1, 7)
UORDER = (2, 1, 3)
MESH = pl.DeviceIdType.MESH


def silu_slope(pre):
    sigma = jax.nn.sigmoid(pre)
    return sigma * (1.0 + pre * (1.0 - sigma))


def kernel(
    x_hbm, w_hbm, cot_hbm, pre_out, grad_out,
    xv, wb, cv, cp, part, sb, zr, us, ur, sl, sg, gs, gr, gl, ls, lr,
    x_sem, cot_sem, own_sem,
    a_send, a_recv, f_send, f_recv,
    z_send, z_recv, u_send, u_recv, s_send, s_recv,
    g_send, g_recv, l_send, l_recv,
):
    table = lax.axis_index("table")
    dp = lax.axis_index("dp")
    u, z = table // NZ, table % NZ
    x, y, c = dp // (NY * NC), (dp // NC) % NY, dp % NC

    def lane(rel, sign, core):
        dx, dy = rel // NY, rel % NY
        px = (x + sign * dx + NX) % NX
        py = (y + dy) % NY
        return (px * NY + py) * NC + core

    def along_z(dz, sign):
        return u * NZ + (z + sign * dz + NZ) % NZ

    def along_u(du, sign):
        return ((u + sign * du + NU) % NU) * NZ + z

    other = 1 - c
    sibling = lane(0, 1, other)

    def to_dp(src, dst, send, recv, peer):
        return pltpu.make_async_remote_copy(
            src_ref=src, dst_ref=dst, send_sem=send, recv_sem=recv,
            device_id=(table, peer), device_id_type=MESH)

    def to_table(src, dst, send, recv, peer):
        return pltpu.make_async_remote_copy(
            src_ref=src, dst_ref=dst, send_sem=send, recv_sem=recv,
            device_id=(peer, dp), device_id_type=MESH)

    x_copy = pltpu.make_async_copy(x_hbm, xv, x_sem)
    x_copy.start()
    cot_copy = pltpu.make_async_copy(cot_hbm, cv, cot_sem)
    cot_copy.start()

    barrier = pltpu.get_barrier_semaphore()
    pl.semaphore_signal(barrier, inc=1, device_id=(table, sibling), device_id_type=MESH)
    for rel in ORDER:
        pl.semaphore_signal(barrier, inc=1, device_id=(table, lane(rel, 1, c)), device_id_type=MESH)
    for dz in ZORDER:
        pl.semaphore_signal(barrier, inc=1, device_id=(along_z(dz, 1), dp), device_id_type=MESH)
    for du in UORDER:
        pl.semaphore_signal(barrier, inc=1, device_id=(along_u(du, 1), dp), device_id_type=MESH)
    pl.semaphore_wait(barrier, 1 + len(ORDER) + len(ZORDER) + len(UORDER))

    def block(ref, h, at):
        return ref.at[h, at]

    def gather_copy(h, rel):
        return to_dp(w_hbm.at[:, pl.ds(h * COLS, COLS)], wb.at[h, dp],
                     a_send.at[h, rel], a_recv.at[h, rel], lane(rel, 1, c))

    def forward_copy(h, rel):
        src = lane(rel, -1, c)
        if rel == 0:
            return to_dp(w_hbm.at[:, pl.ds(h * COLS, COLS)], wb.at[h, dp],
                         f_send.at[h, 0], f_recv.at[h, 0], sibling)
        return to_dp(wb.at[h, src], wb.at[h, src], f_send.at[h, rel], f_recv.at[h, rel], sibling)

    def own_copy(h):
        return pltpu.make_async_copy(w_hbm.at[:, pl.ds(h * COLS, COLS)], wb.at[h, dp], own_sem.at[h])

    def gather_start(h):
        for rel in ORDER:
            gather_copy(h, rel).start()
        forward_copy(h, 0).start()
        own_copy(h).start()

    def add_block(h, src, first=False):
        columns = pl.ds(pl.multiple_of(src * DEPTH, DEPTH), DEPTH)
        product = jnp.dot(xv[:, columns], wb[h, src], preferred_element_type=jnp.float32)
        if first:
            part[h] = product
        else:
            part[h] += product

    def gather_finish(h):
        own_copy(h).wait()
        if h == 0:
            x_copy.wait()
        add_block(h, dp, True)
        for rel in ORDER[::-1]:
            src = lane(rel, -1, c)
            to_dp(wb.at[h, src], wb.at[h, src], a_send.at[h, rel], a_recv.at[h, rel], sibling).wait_recv()
            forward_copy(h, rel).start()
            add_block(h, src)
        for rel in (0,) + ORDER[::-1]:
            src = lane(rel, -1, other)
            to_dp(wb.at[h, src], wb.at[h, src], f_send.at[h, rel], f_recv.at[h, rel], sibling).wait_recv()
            add_block(h, src)

    def z_copy(h, dz):
        return to_table(sb.at[h, (z + dz) % NZ], zr.at[h, dz], z_send.at[h, dz], z_recv.at[h, dz],
                        along_z(dz, 1))

    def z_start(h):
        for at in range(NZ):
            for k in range(NU):
                sb[h, at, k * OWN:(k + 1) * OWN, :] = part[h, (k * NZ + at) * OWN:(k * NZ + at + 1) * OWN, :]
        for dz in ZORDER:
            z_copy(h, dz).start()

    def u_copy(h, du):
        return to_table(us.at[h], ur.at[h, du], u_send.at[h, du], u_recv.at[h, du], along_u(du, 1))

    def z_finish(h):
        total = sb[h, z]
        for dz in ZORDER[::-1]:
            z_copy(h, dz).wait_recv()
            total = total + zr[h, dz]
        us[h] = total
        for du in UORDER:
            u_copy(h, du).start()

    def s_copy(h, dz):
        return to_table(sl.at[h], sg.at[h, z], s_send.at[h, dz], s_recv.at[h, dz], along_z(dz, 1))

    def u_finish(h):
        pre = us[h]
        for du in UORDER[::-1]:
            u_copy(h, du).wait_recv()
            pre = pre + ur[h, du]
        here = slice(h * COLS, (h + 1) * COLS)
        slope = (cp[z, :, here] * silu_slope(pre)).astype(jnp.bfloat16)
        sl[h] = slope
        for dz in ZORDER:
            s_copy(h, dz).start()
        sg[h, z] = slope
        own = pre[0:OWN]
        for k in range(1, NU):
            own = jnp.where(u == k, pre[k * OWN:(k + 1) * OWN], own)
        pre_out[:, here] = own

    def spread(rows, cols):
        i = lax.broadcasted_iota(jnp.int32, (rows, cols), 0)
        j = lax.broadcasted_iota(jnp.int32, (rows, cols), 1)
        k, at, r = i // (NZ * OWN), (i // OWN) % NZ, i % OWN
        return (j == (at * NU + k) * OWN + r).astype(jnp.bfloat16)

    def g_copy(h, rel):
        return to_dp(gs.at[h, rel], gr.at[h, rel], g_send.at[h, rel], g_recv.at[h, rel], sibling)

    def l_copy(h, rel):
        return to_dp(ls.at[h, rel], lr.at[h, rel], l_send.at[h, rel], l_recv.at[h, rel], lane(rel, 1, c))

    def grad_block(slope_t, dst):
        columns = pl.ds(pl.multiple_of(dst * DEPTH, DEPTH), DEPTH)
        return jnp.dot(slope_t, xv[:, columns], preferred_element_type=jnp.float32)

    def grad_start(h):
        for dz in ZORDER[::-1]:
            src = (z + NZ - dz) % NZ
            to_table(sg.at[h, src], sg.at[h, src], s_send.at[h, dz], s_recv.at[h, dz], along_z(dz, 1)).wait_recv()
        packed = sg[h].reshape(ROWS, COLS)
        slope = jnp.dot(spread(ROWS, ROWS), packed, preferred_element_type=jnp.float32)
        slope_t = slope.T.astype(jnp.bfloat16)
        for rel in ORDER + (0,):
            gs[h, rel] = grad_block(slope_t, lane(rel, 1, other)).astype(gs.dtype)
            g_copy(h, rel).start()
        for rel in ORDER + (0,):
            mine = grad_block(slope_t, lane(rel, 1, c))
            g_copy(h, rel).wait_recv()
            mine = mine + gr[h, rel].astype(jnp.float32)
            if rel == 0:
                gl[h] = mine
            else:
                ls[h, rel] = mine.astype(jnp.bfloat16)
                l_copy(h, rel).start()

    def grad_finish(h):
        total = gl[h]
        for rel in ORDER[::-1]:
            l_copy(h, rel).wait_recv()
            total = total + lr[h, rel].astype(jnp.float32)
        grad_out[:, h * COLS:(h + 1) * COLS] = total.T

    gather_start(0)
    gather_start(1)
    cot_copy.wait()
    cot_f32 = cv[...].astype(jnp.float32)
    for at in range(NZ):
        for k in range(NU):
            cp[at, k * OWN:(k + 1) * OWN, :] = cot_f32[(k * NZ + at) * OWN:(k * NZ + at + 1) * OWN, :]
    gather_finish(0)
    z_start(0)
    gather_finish(1)
    z_start(1)
    z_finish(0)
    z_finish(1)
    u_finish(0)
    u_finish(1)
    grad_start(0)
    grad_start(1)
    grad_finish(0)
    grad_finish(1)

    for h in range(HALVES):
        for rel in ORDER:
            gather_copy(h, rel).wait_send()
            l_copy(h, rel).wait_send()
        for rel in (0,) + ORDER:
            forward_copy(h, rel).wait_send()
            g_copy(h, rel).wait_send()
        for dz in ZORDER:
            z_copy(h, dz).wait_send()
            s_copy(h, dz).wait_send()
        for du in UORDER:
            u_copy(h, du).wait_send()


def exchange(features, weight, cotangent):
    bf16, f32 = jnp.bfloat16, jnp.float32
    dma = pltpu.SemaphoreType.DMA
    vmem = pltpu.VMEM
    return pl.pallas_call(
        kernel,
        out_shape=(
            jax.ShapeDtypeStruct((OWN, HALVES * COLS), f32),
            jax.ShapeDtypeStruct((DEPTH, HALVES * COLS), f32),
        ),
        in_specs=[pl.BlockSpec(memory_space=pl.ANY)] * 3,
        out_specs=[pl.BlockSpec(memory_space=pltpu.VMEM)] * 2,
        scratch_shapes=[
            vmem((ROWS, NX * NY * NC * DEPTH), bf16),
            vmem((HALVES, NX * NY * NC, DEPTH, COLS), bf16),
            vmem((ROWS, HALVES * COLS), bf16),
            vmem((NZ, PACK, HALVES * COLS), f32),
            vmem((HALVES, ROWS, COLS), f32),
            vmem((HALVES, NZ, PACK, COLS), f32),
            vmem((HALVES, NZ, PACK, COLS), f32),
            vmem((HALVES, PACK, COLS), f32),
            vmem((HALVES, NU, PACK, COLS), f32),
            vmem((HALVES, PACK, COLS), bf16),
            vmem((HALVES, NZ, PACK, COLS), bf16),
            vmem((HALVES, LANES, COLS, DEPTH), f32),
            vmem((HALVES, LANES, COLS, DEPTH), f32),
            vmem((HALVES, COLS, DEPTH), f32),
            vmem((HALVES, LANES, COLS, DEPTH), bf16),
            vmem((HALVES, LANES, COLS, DEPTH), bf16),
            dma, dma, dma((HALVES,)),
            dma((HALVES, LANES)), dma((HALVES, LANES)), dma((HALVES, LANES)), dma((HALVES, LANES)),
            dma((HALVES, NZ)), dma((HALVES, NZ)), dma((HALVES, NU)), dma((HALVES, NU)),
            dma((HALVES, NZ)), dma((HALVES, NZ)),
            dma((HALVES, LANES)), dma((HALVES, LANES)), dma((HALVES, LANES)), dma((HALVES, LANES)),
        ],
        compiler_params=pltpu.CompilerParams(
            collective_id=0, has_side_effects=True, vmem_limit_bytes=48 * 1024 * 1024
        ),
    )(features, weight, cotangent)


def shards(features, weight, moment_one, moment_two, cotangent):
    pre, grad = exchange(features, weight, cotangent)
    hidden = jax.nn.silu(pre).astype(jnp.bfloat16)
    new_moment_one = 0.9 * moment_one + 0.1 * grad
    new_moment_two = 0.99 * moment_two + 0.01 * grad * grad
    direction = new_moment_one / bias_one / (jnp.sqrt(new_moment_two / bias_two) + 1e-08)
    return (hidden, new_moment_one, new_moment_two, direction)


def solution(mesh):
    return jax.shard_map(
        shards,
        mesh=mesh,
        in_specs=(
            P("dp", "table"),
            P(("table", "dp"), None),
            P(("table", "dp"), None),
            P(("table", "dp"), None),
            P("dp", None),
        ),
        out_specs=(
            P(("dp", "table"), None),
            P(("table", "dp"), None),
            P(("table", "dp"), None),
            P(("table", "dp"), None),
        ),
        check_vma=False,
    )
```

time: 450 us -> 70.2 us (0.16)
  waiting for transfers between devices: 415 us -> 0 us
  Pallas kernels: 0 us -> 63.2 us
  between operations: 13.8 us -> 0.65 us
  matrix products: 7.61 us -> 0 us
  local copies, waits for them, and re-layouts: 8.24 us -> 3.72 us
    psum x1 -> x0, waiting for transfers between devices: 284 us -> none  [shards(): pre_all = lax.psum(partial_value, 'table')]
    reduce_scatter x1 -> x0, waiting for transfers between devices: 83.3 us -> none  [shards(): lax.psum_scatter(lax.dot_general(columns, slope_all, (((0,), (0,)), ((),...]
    pallas_call x0 -> x1, Pallas kernels: none -> 63.2 us  [exchange(): pl.pallas_call(kernel, out_shape=(jax.ShapeDtypeStruct((OWN, HALVES * COL...]
    all_gather x1 -> x0, waiting for transfers between devices: 47.4 us -> none  [shards(): lax.all_gather(weight, 'dp', axis=0, tiled=True)]
    dot_general x2 -> x0, matrix products: 7.61 us -> none  [the longest x1 4.29 us: shards(): lax.dot_general(columns, slope_all, (((0,), (0,)), ((), ())), preferred_e...]
    unnamed x9 -> x10, local copies, waits for them, and re-layouts: 8.24 us -> 3.72 us
  transfers between devices with their start and end apart: 3 -> 0, of which waited for: 3 -> 0; matrix products, arithmetic and copies ran while one was open for 1% -> 0% of each run, Pallas kernels for 0% -> 0%
where the time goes in v1:
time: 70.2 us; the launch traced here: 69.1 us
  Pallas kernels  63.2 us (90%)
  local copies, waits for them, and re-layouts  3.72 us (5%)
  other arithmetic  1.58 us (2%)
    pallas_call x1, Pallas kernels, exchange(): pl.pallas_call(kernel, out_shape=(jax.ShapeDtypeStruct((OWN, HALVES * COL...  63.2 us
    unnamed x10, local copies, waits for them, and re-layouts  3.72 us

profile of v1, /device:TPU:1, one launch (start us, length us, event | category | flops | bytes accessed | tf_op | source)
XLA Modules:
  0.0 69.1 jit_solution(15644866573900226687)
XLA Ops:
  0.6 0.0 copy-start
  0.6 1.9 %copy-done = bf16[384,4096]{1,0:T(8,128)(2,1)S(1)} copy-done((bf16[384,4096]{1,0:T(8,128)(2,1)S(1)}, bf16[384,4096]{1,0:T(8,128)(2,1)}, u32[]{:S(2)}) %copy-start) | copy-done | bytes 3145752
  2.5 0.0 copy-start.1
  2.5 0.9 %copy-done.1 = bf16[384,256]{1,0:T(8,128)(2,1)S(1)} copy-done((bf16[384,256]{1,0:T(8,128)(2,1)S(1)}, bf16[384,256]{1,0:T(8,128)(2,1)}, u32[]{:S(2)}) %copy-start.1) | copy-done | bytes 196632
  3.5 0.0 copy-start.2
  3.5 0.9 %copy-done.2 = bf16[256,256]{1,0:T(8,128)(2,1)S(1)} copy-done((bf16[256,256]{1,0:T(8,128)(2,1)S(1)}, bf16[256,256]{1,0:T(8,128)(2,1)}, u32[]{:S(2)}) %copy-start.2) | copy-done | bytes 131096
  4.4 0.0 copy-start.3
  4.4 0.0 copy-start.4
  4.4 63.2 %shard_map.84 = (f32[12,256]{1,0:T(8,128)S(1)}, f32[256,256]{1,0:T(8,128)S(1)}) custom-call(bf16[384,4096]{1,0:T(8,128)(2,1)S(1)} %copy-done, bf16[256,256]{1,0:T(8,128)(2,1)S(1)} %copy-done.2, bf16[384,256]{1,0:T(8,128)(2,1)S(1)} %copy-done.1), custom_call_target="tpu_custom_call" | custom-call | tf_op jit(solution)/shard_map/pallas_call | solution.py:251
  67.5 0.6 multiply_convert_fusion
  68.2 0.0 copy-done.3
  68.2 0.0 copy-done.4
  68.2 1.0 %add_divide_fusion = (f32[256,256]{1,0:T(8,128)}, f32[256,256]{1,0:T(8,128)}, f32[256,256]{1,0:T(8,128)}) fusion(f32[256,256]{1,0:T(8,128)S(1)} %get-tuple-element.7, f32[256,256]{1,0:T(8,128)S(1)} %copy-done.3, f32[256,256]{1,0:T(8,128)S(1)} %copy-done.4), kind=kLoop, calls=%fused_computation.2 | loop fusion | flops 720896 | bytes 1572864 | tf_op jit(solution)/shard_map/div | solution.py:293
Async XLA Ops:
  0.6 1.9 %copy-start = (bf16[384,4096]{1,0:T(8,128)(2,1)S(1)}, bf16[384,4096]{1,0:T(8,128)(2,1)}, u32[]{:S(2)}) copy-start(bf16[384,4096]{1,0:T(8,128)(2,1)} %x_hbm.1) | copy-start | bytes 9437188
  2.5 0.9 %copy-start.1 = (bf16[384,256]{1,0:T(8,128)(2,1)S(1)}, bf16[384,256]{1,0:T(8,128)(2,1)}, u32[]{:S(2)}) copy-start(bf16[384,256]{1,0:T(8,128)(2,1)} %cot_hbm.1) | copy-start | bytes 589828
  3.5 0.9 %copy-start.2 = (bf16[256,256]{1,0:T(8,128)(2,1)S(1)}, bf16[256,256]{1,0:T(8,128)(2,1)}, u32[]{:S(2)}) copy-start(bf16[256,256]{1,0:T(8,128)(2,1)} %w_hbm.1) | copy-start | bytes 393220
  4.4 63.8 %copy-start.3 = (f32[256,256]{1,0:T(8,128)S(1)}, f32[256,256]{1,0:T(8,128)}, u32[]{:S(2)}) copy-start(f32[256,256]{1,0:T(8,128)} %param.8) | copy-start | bytes 786436
  4.4 63.8 %copy-start.4 = (f32[256,256]{1,0:T(8,128)S(1)}, f32[256,256]{1,0:T(8,128)}, u32[]{:S(2)}) copy-start(f32[256,256]{1,0:T(8,128)} %param.7) | copy-start | bytes 786436

commit v2 on v1

v2 whole, which is shorter than its diff:
```python
import jax
import jax.numpy as jnp
from jax import lax
from jax.experimental import pallas as pl
from jax.experimental.pallas import tpu as pltpu
from jax.sharding import PartitionSpec as P

bias_one = 0.99997343860111
bias_two = 0.63396765872677

NX, NY, NC = 4, 2, 2
NU, NZ = 4, 8
LANES = NX * NY
PARTS, COLS = 4, 64
WIDE = 2 * COLS
ROWS, DEPTH = 384, 256
OWN = ROWS // (NU * NZ)
PACK = OWN * NU // 2
PADDED = 32
ORDER = (5, 4, 3, 7, 2, 6, 1)
ZORDER = (4, 3, 5, 2, 6, 1, 7)
UORDER = (2, 1, 3)
MESH = pl.DeviceIdType.MESH


def silu_slope(pre):
    sigma = jax.nn.sigmoid(pre)
    return sigma * (1.0 + pre * (1.0 - sigma))


def kernel(
    x_hbm, w_hbm, cot_hbm, pre_out, grad_out,
    xv, wv, wb, cv, cp, place, part, packed, own_part, sb, zr, us, ur, sl, sg, own_pre, gs, gr, gl, ls, lr, sums,
    x_sem, cot_sem, own_sem,
    a_send, a_recv, f_send, f_recv,
    z_send, z_recv, u_send, u_recv, s_send, s_recv,
    g_send, g_recv, l_send, l_recv,
):
    table = lax.axis_index("table")
    dp = lax.axis_index("dp")
    u, z = table // NZ, table % NZ
    x, y, c = dp // (NY * NC), (dp // NC) % NY, dp % NC

    def lane(rel, sign, core):
        dx, dy = rel // NY, rel % NY
        px = (x + sign * dx + NX) % NX
        py = (y + dy) % NY
        return (px * NY + py) * NC + core

    def along_z(dz, sign):
        return u * NZ + (z + sign * dz + NZ) % NZ

    def along_u(du, sign):
        return ((u + sign * du + NU) % NU) * NZ + z

    other = 1 - c
    sibling = lane(0, 1, other)

    def to_dp(src, dst, send, recv, peer):
        return pltpu.make_async_remote_copy(
            src_ref=src, dst_ref=dst, send_sem=send, recv_sem=recv,
            device_id=(table, peer), device_id_type=MESH)

    def to_table(src, dst, send, recv, peer):
        return pltpu.make_async_remote_copy(
            src_ref=src, dst_ref=dst, send_sem=send, recv_sem=recv,
            device_id=(peer, dp), device_id_type=MESH)

    w_copy = pltpu.make_async_copy(w_hbm, wv, own_sem)
    w_copy.start()
    x_copy = pltpu.make_async_copy(x_hbm, xv, x_sem)
    x_copy.start()
    cot_copy = pltpu.make_async_copy(cot_hbm, cv, cot_sem)
    cot_copy.start()

    barrier = pltpu.get_barrier_semaphore()
    pl.semaphore_signal(barrier, inc=1, device_id=(table, sibling), device_id_type=MESH)
    for rel in ORDER:
        pl.semaphore_signal(barrier, inc=1, device_id=(table, lane(rel, 1, c)), device_id_type=MESH)
    for dz in ZORDER:
        pl.semaphore_signal(barrier, inc=1, device_id=(along_z(dz, 1), dp), device_id_type=MESH)
    for du in UORDER:
        pl.semaphore_signal(barrier, inc=1, device_id=(along_u(du, 1), dp), device_id_type=MESH)

    def barrier_wait():
        pl.semaphore_wait(barrier, 1 + len(ORDER) + len(ZORDER) + len(UORDER))


    left = lax.broadcasted_iota(jnp.int32, (1, WIDE), 1) < COLS

    def turn(value):
        return pltpu.roll(value, COLS, 1)

    def pack(value, q):
        tile = value[:, q // 2 * WIDE:(q // 2 + 1) * WIDE]
        rows = tile.shape[0] // 2
        first, second = tile[:rows], tile[rows:]
        if q % 2 == 0:
            return jnp.where(left, first, turn(second))
        return jnp.where(left, turn(first), second)

    def gather_copy(q, rel):
        return to_dp(wb.at[q, dp], wb.at[q, dp], a_send.at[q, rel], a_recv.at[q, rel], lane(rel, 1, c))

    def forward_copy(q, rel):
        src = lane(rel, -1, c)
        return to_dp(wb.at[q, src], wb.at[q, src], f_send.at[q, rel], f_recv.at[q, rel], sibling)

    def gather_start(q):
        for rel in ORDER:
            gather_copy(q, rel).start()
        forward_copy(q, 0).start()

    def product(q, src):
        columns = pl.ds(pl.multiple_of(src * DEPTH, DEPTH), DEPTH)
        both = wb[q, src]
        swapped = turn(both.astype(jnp.float32)).astype(jnp.bfloat16)
        return jnp.dot(xv[:, columns], jnp.concatenate([both, swapped], axis=0),
                       preferred_element_type=jnp.float32)

    def gather_finish(q):
        for rel in ORDER[::-1]:
            src = lane(rel, -1, c)
            to_dp(wb.at[q, src], wb.at[q, src], a_send.at[q, rel], a_recv.at[q, rel], sibling).wait_recv()
            forward_copy(q, rel).start()
        part[...] = product(q, dp)
        for rel in ORDER[::-1]:
            part[...] += product(q, lane(rel, -1, c))
        for rel in (0,) + ORDER[::-1]:
            src = lane(rel, -1, other)
            to_dp(wb.at[q, src], wb.at[q, src], f_send.at[q, rel], f_recv.at[q, rel], sibling).wait_recv()
        for rel in (0,) + ORDER[::-1]:
            part[...] += product(q, lane(rel, -1, other))

    def z_copy(h, dz):
        return to_table(sb.at[h, (z + dz) % NZ], zr.at[h, dz], z_send.at[h, dz], z_recv.at[h, dz],
                        along_z(dz, 1))

    def z_start(h):
        half = ROWS // 2
        packed[...] = jnp.where(left, part[0:half], turn(part[half:ROWS]))
        for at in range(NZ):
            for k in range(NU // 2):
                sb[h, at, k * OWN:(k + 1) * OWN, :] = packed[(k * NZ + at) * OWN:(k * NZ + at + 1) * OWN, :]
        for dz in ZORDER:
            z_copy(h, dz).start()

    def u_copy(h, du):
        return to_table(us.at[h], ur.at[h, du], u_send.at[h, du], u_recv.at[h, du], along_u(du, 1))

    def z_finish(h):
        total = sb[h, z]
        for dz in ZORDER[::-1]:
            z_copy(h, dz).wait_recv()
            total = total + zr[h, dz]
        us[h] = total
        for du in UORDER:
            u_copy(h, du).start()

    def s_copy(h, dz):
        return to_table(sl.at[h], sg.at[h, z], s_send.at[h, dz], s_recv.at[h, dz], along_z(dz, 1))

    def u_finish(h):
        pre = us[h]
        for du in UORDER[::-1]:
            u_copy(h, du).wait_recv()
            pre = pre + ur[h, du]
        slope = cp[h, z] * silu_slope(pre)
        slope = jnp.concatenate([slope, jnp.zeros((PADDED - PACK, WIDE), jnp.float32)], axis=0)
        sl[h] = slope.astype(jnp.bfloat16)
        for dz in ZORDER:
            s_copy(h, dz).start()
        sg[h, z] = slope.astype(jnp.bfloat16)
        own = jnp.where(u % 2 == 0, pre[0:OWN], pre[OWN:2 * OWN])
        own_pre[h] = jnp.where(u // 2 == 0, own, turn(own))

    def spread():
        i = lax.broadcasted_iota(jnp.int32, (ROWS, NZ * PADDED), 0)
        j = lax.broadcasted_iota(jnp.int32, (ROWS, NZ * PADDED), 1)
        k, at, r = i // (NZ * OWN) % 2, (i // OWN) % NZ, i % OWN
        return (j == at * PADDED + k * OWN + r).astype(jnp.bfloat16)

    def g_copy(h, rel):
        return to_dp(gs.at[h, rel], gr.at[h, rel], g_send.at[h, rel], g_recv.at[h, rel], sibling)

    def l_copy(h, rel):
        return to_dp(ls.at[h, rel], lr.at[h, rel], l_send.at[h, rel], l_recv.at[h, rel], lane(rel, 1, c))

    def grad_block(slope_t, dst):
        columns = pl.ds(pl.multiple_of(dst * DEPTH, DEPTH), DEPTH)
        return jnp.dot(slope_t, xv[:, columns], preferred_element_type=jnp.float32)

    def grad_start(h):
        for dz in ZORDER[::-1]:
            src = (z + NZ - dz) % NZ
            to_table(sg.at[h, src], sg.at[h, src], s_send.at[h, dz], s_recv.at[h, dz], along_z(dz, 1)).wait_recv()
        slope = jnp.dot(place[...], sg[h].reshape(NZ * PADDED, WIDE), preferred_element_type=jnp.float32).T
        first = lax.broadcasted_iota(jnp.int32, (1, ROWS), 1) < ROWS // 2
        slope_t = jnp.where(first, slope[0:COLS], slope[COLS:WIDE]).astype(jnp.bfloat16)
        for group in (ORDER[:4], ORDER[4:] + (0,)):
            for rel in group:
                gs[h, rel] = grad_block(slope_t, lane(rel, 1, other)).astype(gs.dtype)
            for rel in group:
                g_copy(h, rel).start()
        for rel in ORDER + (0,):
            own_part[rel] = grad_block(slope_t, lane(rel, 1, c))
        for rel in ORDER + (0,):
            g_copy(h, rel).wait_recv()
            mine = own_part[rel] + gr[h, rel].astype(jnp.float32)
            if rel == 0:
                gl[h] = mine
            else:
                ls[h, rel] = mine.astype(jnp.bfloat16)
                l_copy(h, rel).start()

    def grad_finish(h):
        total = gl[h]
        for rel in ORDER[::-1]:
            l_copy(h, rel).wait_recv()
            total = total + lr[h, rel].astype(jnp.float32)
        sums[h % 2 * COLS:(h % 2 + 1) * COLS, :] = total
        if h % 2 == 1:
            grad_out[:, h // 2 * WIDE:(h // 2 + 1) * WIDE] = sums[...].T
            pre_out[:, h // 2 * WIDE:(h // 2 + 1) * WIDE] = jnp.where(left, own_pre[h - 1], turn(own_pre[h]))

    w_copy.wait()
    w_f32 = wv[...].astype(jnp.float32)
    for q in range(PARTS):
        wb[q, dp] = pack(w_f32, q).astype(jnp.bfloat16)
    barrier_wait()
    for q in range(PARTS):
        gather_start(q)
    place[...] = spread()
    cot_copy.wait()
    cot_f32 = cv[...].astype(jnp.float32)
    for q in range(PARTS):
        packed[...] = pack(cot_f32, q)
        for at in range(NZ):
            for k in range(NU // 2):
                cp[q, at, k * OWN:(k + 1) * OWN, :] = packed[(k * NZ + at) * OWN:(k * NZ + at + 1) * OWN, :]
    x_copy.wait()
    gather_finish(0)
    z_start(0)
    gather_finish(1)
    z_start(1)
    gather_finish(2)
    z_start(2)
    z_finish(0)
    gather_finish(3)
    z_start(3)
    z_finish(1)
    z_finish(2)
    u_finish(0)
    z_finish(3)
    u_finish(1)
    u_finish(2)
    grad_start(0)
    u_finish(3)
    grad_start(1)
    grad_start(2)
    grad_start(3)
    for q in range(PARTS):
        grad_finish(q)

    for h in range(PARTS):
        for rel in ORDER:
            gather_copy(h, rel).wait_send()
            l_copy(h, rel).wait_send()
        for rel in (0,) + ORDER:
            forward_copy(h, rel).wait_send()
            g_copy(h, rel).wait_send()
        for dz in ZORDER:
            z_copy(h, dz).wait_send()
            s_copy(h, dz).wait_send()
        for du in UORDER:
            u_copy(h, du).wait_send()


def exchange(features, weight, cotangent):
    bf16, f32 = jnp.bfloat16, jnp.float32
    dma = pltpu.SemaphoreType.DMA
    vmem = pltpu.VMEM
    return pl.pallas_call(
        kernel,
        out_shape=(
            jax.ShapeDtypeStruct((OWN, PARTS * COLS), f32),
            jax.ShapeDtypeStruct((DEPTH, PARTS * COLS), f32),
        ),
        in_specs=[pl.BlockSpec(memory_space=pltpu.HBM)] * 3,
        out_specs=[pl.BlockSpec(memory_space=pltpu.VMEM)] * 2,
        scratch_shapes=[
            vmem((ROWS, NX * NY * NC * DEPTH), bf16),
            vmem((DEPTH, PARTS * COLS), bf16),
            vmem((PARTS, NX * NY * NC, DEPTH // 2, WIDE), bf16),
            vmem((ROWS, PARTS * COLS), bf16),
            vmem((PARTS, NZ, PACK, WIDE), f32),
            vmem((ROWS, NZ * PADDED), bf16),
            vmem((ROWS, WIDE), f32),
            vmem((ROWS // 2, WIDE), f32),
            vmem((LANES, COLS, DEPTH), f32),
            vmem((PARTS, NZ, PACK, WIDE), f32),
            vmem((PARTS, NZ, PACK, WIDE), f32),
            vmem((PARTS, PACK, WIDE), f32),
            vmem((PARTS, NU, PACK, WIDE), f32),
            vmem((PARTS, PADDED, WIDE), bf16),
            vmem((PARTS, NZ, PADDED, WIDE), bf16),
            vmem((PARTS, OWN, WIDE), f32),
            vmem((PARTS, LANES, COLS, DEPTH), bf16),
            vmem((PARTS, LANES, COLS, DEPTH), bf16),
            vmem((PARTS, COLS, DEPTH), f32),
            vmem((PARTS, LANES, COLS, DEPTH), bf16),
            vmem((PARTS, LANES, COLS, DEPTH), bf16),
            vmem((WIDE, DEPTH), f32),
            dma, dma, dma,
            dma((PARTS, LANES)), dma((PARTS, LANES)), dma((PARTS, LANES)), dma((PARTS, LANES)),
            dma((PARTS, NZ)), dma((PARTS, NZ)), dma((PARTS, NU)), dma((PARTS, NU)),
            dma((PARTS, NZ)), dma((PARTS, NZ)),
            dma((PARTS, LANES)), dma((PARTS, LANES)), dma((PARTS, LANES)), dma((PARTS, LANES)),
        ],
        compiler_params=pltpu.CompilerParams(
            collective_id=0, has_side_effects=True, vmem_limit_bytes=48 * 1024 * 1024
        ),
    )(*(pltpu.with_memory_space_constraint(a, pltpu.HBM) for a in (features, weight, cotangent)))


def shards(features, weight, moment_one, moment_two, cotangent):
    pre, grad = exchange(features, weight, cotangent)
    hidden = jax.nn.silu(pre).astype(jnp.bfloat16)
    new_moment_one = 0.9 * moment_one + 0.1 * grad
    new_moment_two = 0.99 * moment_two + 0.01 * grad * grad
    direction = new_moment_one / bias_one / (jnp.sqrt(new_moment_two / bias_two) + 1e-08)
    return (hidden, new_moment_one, new_moment_two, direction)


def solution(mesh):
    return jax.shard_map(
        shards,
        mesh=mesh,
        in_specs=(
            P("dp", "table"),
            P(("table", "dp"), None),
            P(("table", "dp"), None),
            P(("table", "dp"), None),
            P("dp", None),
        ),
        out_specs=(
            P(("dp", "table"), None),
            P(("table", "dp"), None),
            P(("table", "dp"), None),
            P(("table", "dp"), None),
        ),
        check_vma=False,
    )
```

time: 70.2 us -> 61.4 us (0.87); the launches traced: 69.1 us -> 61.3 us
  Pallas kernels: 63.2 us -> 59 us
  local copies, waits for them, and re-layouts: 3.72 us -> 0.01 us
    pallas_call x1, Pallas kernels: 63.2 us -> 59 us  [exchange(): pl.pallas_call(kernel, out_shape=(jax.ShapeDtypeStruct((OWN, PARTS * COLS...]
    unnamed x10 -> x4, local copies, waits for them, and re-layouts: 3.72 us -> 0.01 us
where the time goes in v2:
time: 61.4 us; the launch traced here: 61.3 us
  Pallas kernels  59 us (96%)
  other arithmetic  1.58 us (3%)
  between operations  0.66 us (1%)
    pallas_call x1, Pallas kernels, exchange(): pl.pallas_call(kernel, out_shape=(jax.ShapeDtypeStruct((OWN, PARTS * COLS...  59 us

profile of v2, /device:TPU:1, one launch (start us, length us, event | category | flops | bytes accessed | tf_op | source)
XLA Modules:
  0.0 61.3 jit_solution(1810194948063080048)
XLA Ops:
  0.6 0.0 copy-start
  0.6 0.0 copy-start.1
  0.7 59.0 %shard_map.84 = (f32[12,256]{1,0:T(8,128)S(1)}, f32[256,256]{1,0:T(8,128)S(1)}) custom-call(bf16[384,4096]{1,0:T(8,128)(2,1)} %x_hbm.1, bf16[256,256]{1,0:T(8,128)(2,1)} %w_hbm.1, bf16[384,256]{1,0:T(8,128)(2,1)} %cot_hbm.1), custom_call_target="tpu_custom_call" | custom-call | tf_op jit(solution)/shard_map/pallas_call | solution.py:283
  59.7 0.6 %multiply_convert_fusion = bf16[12,256]{1,0:T(8,128)(2,1)} fusion(f32[12,256]{1,0:T(8,128)S(1)} %get-tuple-element.6), kind=kLoop, calls=%fused_computation.4 | loop fusion | flops 15360 | bytes 18432 | tf_op jit(solution)/shard_map/convert_element_type | solution.py:328
  60.3 0.0 copy-done
  60.3 0.0 copy-done.1
  60.3 1.0 %add_divide_fusion = (f32[256,256]{1,0:T(8,128)}, f32[256,256]{1,0:T(8,128)}, f32[256,256]{1,0:T(8,128)}) fusion(f32[256,256]{1,0:T(8,128)S(1)} %get-tuple-element.7, f32[256,256]{1,0:T(8,128)S(1)} %copy-done, f32[256,256]{1,0:T(8,128)S(1)} %copy-done.1), kind=kLoop, calls=%fused_computation.2 | loop fusion | flops 720896 | bytes 1572864 | tf_op jit(solution)/shard_map/div | solution.py:331
Async XLA Ops:
  0.6 59.7 %copy-start = (f32[256,256]{1,0:T(8,128)S(1)}, f32[256,256]{1,0:T(8,128)}, u32[]{:S(2)}) copy-start(f32[256,256]{1,0:T(8,128)} %param.8) | copy-start | bytes 786436
  0.6 59.7 %copy-start.1 = (f32[256,256]{1,0:T(8,128)S(1)}, f32[256,256]{1,0:T(8,128)}, u32[]{:S(2)}) copy-start(f32[256,256]{1,0:T(8,128)} %param.7) | copy-start | bytes 786436

commit v3 on v2

--- a/solution.py
+++ b/solution.py
@@ -18,6 +18,7 @@
 PACK = OWN * NU // 2
 PADDED = 32
 ORDER = (5, 4, 3, 7, 2, 6, 1)
+BOTH = 2 * ROWS
 ZORDER = (4, 3, 5, 2, 6, 1, 7)
 UORDER = (2, 1, 3)
 MESH = pl.DeviceIdType.MESH
@@ -30,9 +31,9 @@
 
 def kernel(
     x_hbm, w_hbm, cot_hbm, pre_out, grad_out,
-    xv, wv, wb, cv, cp, place, part, packed, own_part, sb, zr, us, ur, sl, sg, own_pre, gs, gr, gl, ls, lr, sums,
-    x_sem, cot_sem, own_sem,
-    a_send, a_recv, f_send, f_recv,
+    xv, wv, wb, cv, cp, place, part, packed, pair_out, pair_in, sb, zr, us, ur, sl, sg, own_pre, mine, theirs, gl, ls, lr, sums,
+    x_sem, cot_sem, own_sem, swap_send, swap_recv,
+    a_send, a_recv, pair_send, pair_recv,
     z_send, z_recv, u_send, u_recv, s_send, s_recv,
     g_send, g_recv, l_send, l_recv,
 ):
@@ -41,6 +42,9 @@
     u, z = table // NZ, table % NZ
     x, y, c = dp // (NY * NC), (dp // NC) % NY, dp % NC
 
+    def chip_at(rel, sign):
+        return (x + sign * (rel // NY) + NX) % NX * NY + (y + rel % NY) % NY
+
     def lane(rel, sign, core):
         dx, dy = rel // NY, rel % NY
         px = (x + sign * dx + NX) % NX
@@ -68,8 +72,15 @@
 
     w_copy = pltpu.make_async_copy(w_hbm, wv, own_sem)
     w_copy.start()
-    x_copy = pltpu.make_async_copy(x_hbm, xv, x_sem)
-    x_copy.start()
+
+    def x_copy(k):
+        columns = pl.ds(pl.multiple_of((k * NC + c) * DEPTH, DEPTH), DEPTH)
+        return pltpu.make_async_copy(x_hbm.at[:, columns], xv.at[k, pl.ds(0, ROWS)], x_sem.at[k])
+
+    def x_swap(k):
+        columns = pl.ds(pl.multiple_of((k * NC + other) * DEPTH, DEPTH), DEPTH)
+        return to_dp(x_hbm.at[:, columns], xv.at[k, pl.ds(ROWS, ROWS)], swap_send.at[k], swap_recv.at[k], sibling)
+
     cot_copy = pltpu.make_async_copy(cot_hbm, cv, cot_sem)
     cot_copy.start()
 
@@ -100,48 +111,49 @@
         return jnp.where(left, turn(first), second)
 
     def gather_copy(q, rel):
-        return to_dp(wb.at[q, dp], wb.at[q, dp], a_send.at[q, rel], a_recv.at[q, rel], lane(rel, 1, c))
-
-    def forward_copy(q, rel):
-        src = lane(rel, -1, c)
-        return to_dp(wb.at[q, src], wb.at[q, src], f_send.at[q, rel], f_recv.at[q, rel], sibling)
+        return to_dp(wb.at[q, chip_at(0, 1)], wb.at[q, chip_at(0, 1)], a_send.at[q, rel], a_recv.at[q, rel], lane(rel, 1, c))
 
     def gather_start(q):
         for rel in ORDER:
             gather_copy(q, rel).start()
-        forward_copy(q, 0).start()
-
-    def product(q, src):
-        columns = pl.ds(pl.multiple_of(src * DEPTH, DEPTH), DEPTH)
-        both = wb[q, src]
-        swapped = turn(both.astype(jnp.float32)).astype(jnp.bfloat16)
-        return jnp.dot(xv[:, columns], jnp.concatenate([both, swapped], axis=0),
-                       preferred_element_type=jnp.float32)
+
+    def product(q, chip):
+        block = wb[q, chip]
+        swapped = turn(block.astype(jnp.float32)).astype(jnp.bfloat16)
+        return jnp.dot(xv[chip], jnp.concatenate([block, swapped], axis=0), preferred_element_type=jnp.float32)
+
+    def pair_copy(q):
+        return to_dp(pair_out.at[q], pair_in.at[q], pair_send.at[q], pair_recv.at[q], sibling)
+
+    def two_groups(rows):
+        half = ROWS // 2
+        return jnp.where(left, part[rows:rows + half], turn(part[rows + half:rows + ROWS]))
 
     def gather_finish(q):
-        for rel in ORDER[::-1]:
-            src = lane(rel, -1, c)
-            to_dp(wb.at[q, src], wb.at[q, src], a_send.at[q, rel], a_recv.at[q, rel], sibling).wait_recv()
-            forward_copy(q, rel).start()
-        part[...] = product(q, dp)
-        for rel in ORDER[::-1]:
-            part[...] += product(q, lane(rel, -1, c))
-        for rel in (0,) + ORDER[::-1]:
-            src = lane(rel, -1, other)
-            to_dp(wb.at[q, src], wb.at[q, src], f_send.at[q, rel], f_recv.at[q, rel], sibling).wait_recv()
-        for rel in (0,) + ORDER[::-1]:
-            part[...] += product(q, lane(rel, -1, other))
+        for group in (ORDER[:4], ORDER[4:]):
+            for rel in group:
+                src = chip_at(rel, -1)
+                to_dp(wb.at[q, src], wb.at[q, src], a_send.at[q, rel], a_recv.at[q, rel], sibling).wait_recv()
+            if group == ORDER[:4]:
+                part[...] = product(q, chip_at(0, 1))
+            elif q + 2 < PARTS:
+                gather_start(q + 2)
+            for rel in group:
+                part[...] += product(q, chip_at(rel, -1))
+        pair_out[q] = two_groups(ROWS)
+        pair_copy(q).start()
+        packed[q] = two_groups(0)
 
     def z_copy(h, dz):
         return to_table(sb.at[h, (z + dz) % NZ], zr.at[h, dz], z_send.at[h, dz], z_recv.at[h, dz],
                         along_z(dz, 1))
 
     def z_start(h):
-        half = ROWS // 2
-        packed[...] = jnp.where(left, part[0:half], turn(part[half:ROWS]))
+        pair_copy(h).wait_recv()
+        packed[h] += pair_in[h]
         for at in range(NZ):
             for k in range(NU // 2):
-                sb[h, at, k * OWN:(k + 1) * OWN, :] = packed[(k * NZ + at) * OWN:(k * NZ + at + 1) * OWN, :]
+                sb[h, at, k * OWN:(k + 1) * OWN, :] = packed[h, (k * NZ + at) * OWN:(k * NZ + at + 1) * OWN, :]
         for dz in ZORDER:
             z_copy(h, dz).start()
 
@@ -180,15 +192,11 @@
         k, at, r = i // (NZ * OWN) % 2, (i // OWN) % NZ, i % OWN
         return (j == at * PADDED + k * OWN + r).astype(jnp.bfloat16)
 
-    def g_copy(h, rel):
-        return to_dp(gs.at[h, rel], gr.at[h, rel], g_send.at[h, rel], g_recv.at[h, rel], sibling)
+    def g_copy(h):
+        return to_dp(mine.at[h], theirs.at[h], g_send.at[h], g_recv.at[h], sibling)
 
     def l_copy(h, rel):
         return to_dp(ls.at[h, rel], lr.at[h, rel], l_send.at[h, rel], l_recv.at[h, rel], lane(rel, 1, c))
-
-    def grad_block(slope_t, dst):
-        columns = pl.ds(pl.multiple_of(dst * DEPTH, DEPTH), DEPTH)
-        return jnp.dot(slope_t, xv[:, columns], preferred_element_type=jnp.float32)
 
     def grad_start(h):
         for dz in ZORDER[::-1]:
@@ -196,22 +204,22 @@
             to_table(sg.at[h, src], sg.at[h, src], s_send.at[h, dz], s_recv.at[h, dz], along_z(dz, 1)).wait_recv()
         slope = jnp.dot(place[...], sg[h].reshape(NZ * PADDED, WIDE), preferred_element_type=jnp.float32).T
         first = lax.broadcasted_iota(jnp.int32, (1, ROWS), 1) < ROWS // 2
-        slope_t = jnp.where(first, slope[0:COLS], slope[COLS:WIDE]).astype(jnp.bfloat16)
-        for group in (ORDER[:4], ORDER[4:] + (0,)):
+        mine[h] = jnp.where(first, slope[0:COLS], slope[COLS:WIDE]).astype(jnp.bfloat16)
+        g_copy(h).start()
+
+    def grad_send(h):
+        g_copy(h).wait_recv()
+        slope_t = jnp.concatenate([mine[h], theirs[h]], axis=1)
+        for group in ((5, 4), (3, 7), (2, 6), (1, 0)):
             for rel in group:
-                gs[h, rel] = grad_block(slope_t, lane(rel, 1, other)).astype(gs.dtype)
+                block = jnp.dot(slope_t, xv[chip_at(rel, 1)], preferred_element_type=jnp.float32)
+                if rel == 0:
+                    gl[h] = block
+                else:
+                    ls[h, rel] = block.astype(jnp.bfloat16)
             for rel in group:
-                g_copy(h, rel).start()
-        for rel in ORDER + (0,):
-            own_part[rel] = grad_block(slope_t, lane(rel, 1, c))
-        for rel in ORDER + (0,):
-            g_copy(h, rel).wait_recv()
-            mine = own_part[rel] + gr[h, rel].astype(jnp.float32)
-            if rel == 0:
-                gl[h] = mine
-            else:
-                ls[h, rel] = mine.astype(jnp.bfloat16)
-                l_copy(h, rel).start()
+                if rel != 0:
+                    l_copy(h, rel).start()
 
     def grad_finish(h):
         total = gl[h]
@@ -223,22 +231,29 @@
             grad_out[:, h // 2 * WIDE:(h // 2 + 1) * WIDE] = sums[...].T
             pre_out[:, h // 2 * WIDE:(h // 2 + 1) * WIDE] = jnp.where(left, own_pre[h - 1], turn(own_pre[h]))
 
+    for k in range(LANES):
+        x_copy(k).start()
     w_copy.wait()
     w_f32 = wv[...].astype(jnp.float32)
     for q in range(PARTS):
-        wb[q, dp] = pack(w_f32, q).astype(jnp.bfloat16)
+        wb[q, chip_at(0, 1)] = pack(w_f32, q).astype(jnp.bfloat16)
     barrier_wait()
-    for q in range(PARTS):
+    gather_start(0)
+    for k in range(LANES):
+        x_swap(k).start()
+    for q in range(1, 2):
         gather_start(q)
     place[...] = spread()
     cot_copy.wait()
     cot_f32 = cv[...].astype(jnp.float32)
     for q in range(PARTS):
-        packed[...] = pack(cot_f32, q)
+        packed[q] = pack(cot_f32, q)
         for at in range(NZ):
             for k in range(NU // 2):
-                cp[q, at, k * OWN:(k + 1) * OWN, :] = packed[(k * NZ + at) * OWN:(k * NZ + at + 1) * OWN, :]
-    x_copy.wait()
+                cp[q, at, k * OWN:(k + 1) * OWN, :] = packed[q, (k * NZ + at) * OWN:(k * NZ + at + 1) * OWN, :]
+    for k in range(LANES):
+        x_copy(k).wait()
+        x_swap(k).wait_recv()
     gather_finish(0)
     z_start(0)
     gather_finish(1)
@@ -249,31 +264,41 @@
     gather_finish(3)
     z_start(3)
     z_finish(1)
+    u_finish(0)
     z_finish(2)
-    u_finish(0)
+    u_finish(1)
     z_finish(3)
-    u_finish(1)
+    grad_start(0)
     u_finish(2)
-    grad_start(0)
+    grad_send(0)
+    grad_start(1)
+    grad_send(1)
     u_finish(3)
-    grad_start(1)
     grad_start(2)
+    grad_send(2)
+    grad_finish(0)
     grad_start(3)
-    for q in range(PARTS):
-        grad_finish(q)
-
+    grad_finish(1)
+    grad_send(3)
+    grad_finish(2)
+    for k in range(LANES):
+        x_swap(k).wait_send()
     for h in range(PARTS):
         for rel in ORDER:
             gather_copy(h, rel).wait_send()
-            l_copy(h, rel).wait_send()
-        for rel in (0,) + ORDER:
-            forward_copy(h, rel).wait_send()
-            g_copy(h, rel).wait_send()
+            if h < PARTS - 1:
+                l_copy(h, rel).wait_send()
+        pair_copy(h).wait_send()
+        g_copy(h).wait_send()
         for dz in ZORDER:
             z_copy(h, dz).wait_send()
             s_copy(h, dz).wait_send()
         for du in UORDER:
             u_copy(h, du).wait_send()
+    grad_finish(3)
+
+    for rel in ORDER:
+        l_copy(PARTS - 1, rel).wait_send()
 
 
 def exchange(features, weight, cotangent):
@@ -289,15 +314,16 @@
         in_specs=[pl.BlockSpec(memory_space=pltpu.HBM)] * 3,
         out_specs=[pl.BlockSpec(memory_space=pltpu.VMEM)] * 2,
         scratch_shapes=[
-            vmem((ROWS, NX * NY * NC * DEPTH), bf16),
+            vmem((LANES, BOTH, DEPTH), bf16),
             vmem((DEPTH, PARTS * COLS), bf16),
-            vmem((PARTS, NX * NY * NC, DEPTH // 2, WIDE), bf16),
+            vmem((PARTS, LANES, DEPTH // 2, WIDE), bf16),
             vmem((ROWS, PARTS * COLS), bf16),
             vmem((PARTS, NZ, PACK, WIDE), f32),
             vmem((ROWS, NZ * PADDED), bf16),
-            vmem((ROWS, WIDE), f32),
-            vmem((ROWS // 2, WIDE), f32),
-            vmem((LANES, COLS, DEPTH), f32),
+            vmem((BOTH, WIDE), f32),
+            vmem((PARTS, ROWS // 2, WIDE), f32),
+            vmem((PARTS, ROWS // 2, WIDE), f32),
+            vmem((PARTS, ROWS // 2, WIDE), f32),
             vmem((PARTS, NZ, PACK, WIDE), f32),
             vmem((PARTS, NZ, PACK, WIDE), f32),
             vmem((PARTS, PACK, WIDE), f32),
@@ -305,17 +331,17 @@
             vmem((PARTS, PADDED, WIDE), bf16),
             vmem((PARTS, NZ, PADDED, WIDE), bf16),
             vmem((PARTS, OWN, WIDE), f32),
-            vmem((PARTS, LANES, COLS, DEPTH), bf16),
-            vmem((PARTS, LANES, COLS, DEPTH), bf16),
+            vmem((PARTS, COLS, ROWS), bf16),
+            vmem((PARTS, COLS, ROWS), bf16),
             vmem((PARTS, COLS, DEPTH), f32),
             vmem((PARTS, LANES, COLS, DEPTH), bf16),
             vmem((PARTS, LANES, COLS, DEPTH), bf16),
             vmem((WIDE, DEPTH), f32),
-            dma, dma, dma,
-            dma((PARTS, LANES)), dma((PARTS, LANES)), dma((PARTS, LANES)), dma((PARTS, LANES)),
+            dma((LANES,)), dma, dma, dma((LANES,)), dma((LANES,)),
+            dma((PARTS, LANES)), dma((PARTS, LANES)), dma((PARTS,)), dma((PARTS,)),
             dma((PARTS, NZ)), dma((PARTS, NZ)), dma((PARTS, NU)), dma((PARTS, NU)),
             dma((PARTS, NZ)), dma((PARTS, NZ)),
-            dma((PARTS, LANES)), dma((PARTS, LANES)), dma((PARTS, LANES)), dma((PARTS, LANES)),
+            dma((PARTS,)), dma((PARTS,)), dma((PARTS, LANES)), dma((PARTS, LANES)),
         ],
         compiler_params=pltpu.CompilerParams(
             collective_id=0, has_side_effects=True, vmem_limit_bytes=48 * 1024 * 1024

time: 61.4 us -> 61.6 us (level)
  no operation moved by 1% of the time
where the time goes in v3:
time: 61.6 us; the launch traced here: 61.5 us
  Pallas kernels  59.2 us (96%)
  other arithmetic  1.58 us (3%)
  between operations  0.66 us (1%)
    pallas_call x1, Pallas kernels, exchange(): pl.pallas_call(kernel, out_shape=(jax.ShapeDtypeStruct((OWN, PARTS * COLS...  59.2 us

profile of v3, /device:TPU:1, one launch (start us, length us, event | category | flops | bytes accessed | tf_op | source)
XLA Modules:
  0.0 61.5 jit_solution(5972728350009313813)
XLA Ops:
  0.6 0.0 copy-start
  0.6 0.0 copy-start.1
  0.7 59.2 %shard_map.84 = (f32[12,256]{1,0:T(8,128)S(1)}, f32[256,256]{1,0:T(8,128)S(1)}) custom-call(bf16[384,4096]{1,0:T(8,128)(2,1)} %x_hbm.1, bf16[256,256]{1,0:T(8,128)(2,1)} %w_hbm.1, bf16[384,256]{1,0:T(8,128)(2,1)} %cot_hbm.1), custom_call_target="tpu_custom_call" | custom-call | tf_op jit(solution)/shard_map/pallas_call | solution.py:308
  59.9 0.6 %multiply_convert_fusion = bf16[12,256]{1,0:T(8,128)(2,1)} fusion(f32[12,256]{1,0:T(8,128)S(1)} %get-tuple-element.6), kind=kLoop, calls=%fused_computation.4 | loop fusion | flops 15360 | bytes 18432 | tf_op jit(solution)/shard_map/convert_element_type | solution.py:354
  60.5 0.0 copy-done
  60.5 0.0 copy-done.1
  60.5 1.0 %add_divide_fusion = (f32[256,256]{1,0:T(8,128)}, f32[256,256]{1,0:T(8,128)}, f32[256,256]{1,0:T(8,128)}) fusion(f32[256,256]{1,0:T(8,128)S(1)} %get-tuple-element.7, f32[256,256]{1,0:T(8,128)S(1)} %copy-done, f32[256,256]{1,0:T(8,128)S(1)} %copy-done.1), kind=kLoop, calls=%fused_computation.2 | loop fusion | flops 720896 | bytes 1572864 | tf_op jit(solution)/shard_map/div | solution.py:357
Async XLA Ops:
  0.6 59.9 %copy-start = (f32[256,256]{1,0:T(8,128)S(1)}, f32[256,256]{1,0:T(8,128)}, u32[]{:S(2)}) copy-start(f32[256,256]{1,0:T(8,128)} %param.8) | copy-start | bytes 786436
  0.6 59.9 %copy-start.1 = (f32[256,256]{1,0:T(8,128)S(1)}, f32[256,256]{1,0:T(8,128)}, u32[]{:S(2)}) copy-start(f32[256,256]{1,0:T(8,128)} %param.7) | copy-start | bytes 786436
